TPU v7x, 32 devices: a whole 2x2x4 slice. The times are simulated.
32 devices in a mesh: dp: 8 (over z, x), blk: 4 (over y, core).
Axes of the slice: x: 2, y: 2, z: 4, core: 2. Of those that a mesh axis runs over, the one named last changes fastest.
Arguments:
- hidden_pre: bfloat16 [1536, 24576], P('dp', 'blk'), may hold values from -6 to 6
- out_grad: bfloat16 [1536, 6144], P('dp', 'blk'), may hold values from -6 to 6
- w_up_blocks: bfloat16 [1152, 128, 128], P('blk'), may hold values from -0.109375 to 0.109375
- up_index: int32 [1152, 2], P('blk'), may hold values from 0 to 47, as said below
- w_down_blocks: bfloat16 [1152, 128, 128], P('blk'), may hold values from -0.21875 to 0.21875
- down_index: int32 [1152, 2], P('blk'), may hold values from 0 to 47, as said below
Outputs:
- in_grad: bfloat16 [1536, 6144], P('dp', 'blk')
- w_down_grad: float32 [147456, 128], P(('blk', 'dp'))
Inputs may be any that keep to these rules, and one draw needn't show every extreme that they name: `up_index`: each run of 288 rows that starts at a multiple of 288 belongs to one shard and lists distinct pairs (r, c) with r below 48 and c below 48; every shard holds the pair (47, 47). `down_index`: each run of 288 rows that starts at a multiple of 288 belongs to one shard and lists distinct pairs (r, c) with r below 48 and c below 48; every shard holds the pair (47, 47).
All inputs are finite; a program needn't handle non-finite values.
Results may differ from a plain program's by a relative error of at most 0.014.
Values may be sent and summed in bfloat16 or wider, within the bound.
A program may use at most 192 MiB of HBM per device.

v0:
```python
import jax
import jax.numpy as jnp
from jax import lax
from jax.sharding import PartitionSpec as P

inv_root_two = 0.7071067811865476
inv_root_twopi = 0.3989422804014327


def local(hidden_pre, out_grad, w_up_blocks, up_index, w_down_blocks, down_index):
    tok_rows, hid_width = hidden_pre.shape
    block_size = w_up_blocks.shape[1]
    hid_blocks = hid_width // block_size
    grad_scale = float((tok_rows * lax.axis_size("dp")) ** (-0.5))
    full_grad = lax.all_gather(out_grad, "blk", axis=1, tiled=True)
    feat_blocks = full_grad.shape[1] // block_size
    pre_float = hidden_pre.astype(jnp.float32)
    normal_cdf = 0.5 * (1.0 + lax.erf(pre_float * inv_root_two))
    gelu_slope = normal_cdf + pre_float * jnp.exp(-0.5 * pre_float * pre_float) * inv_root_twopi
    activation = (pre_float * normal_cdf).astype(jnp.bfloat16)
    grad_panels = jnp.take(
        full_grad.reshape(tok_rows, feat_blocks, block_size), down_index[:, 0], axis=1
    )
    down_terms = jnp.einsum(
        "tbj,bij->tbi", grad_panels, w_down_blocks, preferred_element_type=jnp.float32
    )
    hid_ids = jnp.arange(hid_blocks, dtype=jnp.int32)
    down_pick = (down_index[:, 1][:, None] == hid_ids[None, :]).astype(jnp.float32)
    act_grad = jnp.einsum("tbi,bf->tfi", down_terms, down_pick).reshape(tok_rows, hid_width)
    pre_grad = (act_grad * gelu_slope).astype(jnp.bfloat16)
    pre_panels = jnp.take(
        pre_grad.reshape(tok_rows, hid_blocks, block_size), up_index[:, 1], axis=1
    )
    up_terms = jnp.einsum(
        "tbi,bji->tbj", pre_panels, w_up_blocks, preferred_element_type=jnp.float32
    )
    feat_ids = jnp.arange(feat_blocks, dtype=jnp.int32)
    up_pick = (up_index[:, 0][:, None] == feat_ids[None, :]).astype(jnp.float32)
    partial_sum = jnp.einsum("tbj,bd->tdj", up_terms, up_pick).reshape(
        tok_rows, feat_blocks * block_size
    )
    summed = lax.psum_scatter(
        partial_sum.astype(jnp.bfloat16), "blk", scatter_dimension=1, tiled=True
    )
    act_panels = jnp.take(
        activation.reshape(tok_rows, hid_blocks, block_size), down_index[:, 1], axis=1
    )
    local_grad = (
        jnp.einsum("tbi,tbj->bij", act_panels, grad_panels, preferred_element_type=jnp.float32)
        * grad_scale
    )
    weight_out = lax.psum_scatter(
        local_grad.reshape(-1, block_size), "dp", scatter_dimension=0, tiled=True
    )
    return (summed, weight_out)


def solution(mesh):
    placed = (
        P("dp", "blk"),
        P("dp", "blk"),
        P("blk", None, None),
        P("blk", None),
        P("blk", None, None),
        P("blk", None),
    )
    return jax.shard_map(
        local,
        mesh=mesh,
        in_specs=placed,
        out_specs=(P("dp", "blk"), P(("blk", "dp"), None)),
        check_vma=False,
    )
```

profile of v0, /device:TPU:8, one launch (start us, length us, event | category | flops | bytes accessed | tf_op | source)
XLA Modules:
  0.0 491.2 jit_solution(11907931831916348377)
XLA Ops:
  7.2 0.0 all-gather.2.cloned.1.call-start
  7.2 0.7 all-gather.2.cloned.1.call-update
  7.9 0.0 reduce-scatter.3.cloned.1.call-start
  7.9 0.8 slice_reduce_fusion.3
  8.7 0.8 slice_reduce_fusion.2
  9.6 25.2 %all-gather.2.cloned.1.call-done = bf16[192,6144]{1,0:T(8,128)(2,1)} async-done(((bf16[192,1536]{1,0:T(8,128)(2,1)}), bf16[192,6144]{1,0:T(8,128)(2,1)}) %all-gather.2.cloned.1.call-update) | async-done | bytes 2359312 | tf_op jit(solution)/shard_map/all_gather | solution.py:15
  34.8 2.3 copy_bitcast_fusion.3
  37.2 12.1 %gather_fusion = bf16[288,192,128]{2,1,0:T(8,128)(2,1)} fusion(bf16[192,48,128]{2,0,1:T(8,128)(2,1)S(1)} %copy_bitcast_fusion.3, s32[1024]{0:T(1024)S(1)} %pad_clamp_fusion.2), kind=kCustom, calls=%fused_computation.clone | custom fusion | bytes 28312704 | tf_op jit(solution)/shard_map/jit(_take)/gather | solution.py:21
  49.3 16.5 %fusion.18 = bf16[192,288,128]{2,0,1:T(8,128)(2,1)} fusion(bf16[288,128,128]{2,1,0:T(8,128)(2,1)} %param.12, bf16[288,192,128]{2,1,0:T(8,128)(2,1)} %gather_fusion, pred[288]{0:T(512)(128)(4,1)S(1)} %get-tuple-element.10), kind=kOutput, calls=%fused_computation.20 | convolution fusion | flops 1819017216 | bytes 37749024 | tf_op jit(solution)/shard_map/tbj,bij->tbi/dot_general | solution.py:24
  65.8 0.0 copy-start
  65.8 19.6 %fusion.2 = f32[48,192,128]{2,0,1:T(8,128)S(1)} fusion(bf16[192,288,128]{2,0,1:T(8,128)(2,1)} %fusion.18, s32[288]{0:T(512)S(1)} %get-tuple-element.5), kind=kOutput, calls=%fused_computation.5 | convolution fusion | flops 679491072 | bytes 18875520 | tf_op jit(solution)/shard_map/tbi,bf->tfi/dot_general | solution.py:29
  85.4 0.0 copy-done
  85.4 3.9 fusion.36
  89.3 0.7 copy.33
  90.0 12.5 %gather_fusion.1 = bf16[288,192,128]{2,1,0:T(8,128)(2,1)} fusion(bf16[192,48,128]{2,0,1:T(8,128)(2,1)S(1)} %bitcast.58, s32[1024]{0:T(1024)S(1)} %pad_clamp_fusion.1), kind=kCustom, calls=%fused_computation.1.clone | custom fusion | bytes 28312704 | tf_op jit(solution)/shard_map/jit(_take)/gather | solution.py:31
  102.4 16.5 %fusion.15 = bf16[192,288,128]{2,0,1:T(8,128)(2,1)} fusion(bf16[288,128,128]{2,1,0:T(8,128)(2,1)} %param.10, bf16[288,192,128]{2,1,0:T(8,128)(2,1)} %gather_fusion.1, pred[288]{0:T(512)(128)(4,1)S(1)} %compare_and_fusion.1), kind=kOutput, calls=%fused_computation.19 | convolution fusion | flops 1819017216 | bytes 37749024 | tf_op jit(solution)/shard_map/tbi,bji->tbj/dot_general | solution.py:34
  118.9 13.6 %fusion.38 = bf16[48,192,128]{2,0,1:T(8,128)(2,1)S(1)} fusion(bf16[192,288,128]{2,0,1:T(8,128)(2,1)} %fusion.15, s32[288]{0:T(512)S(1)} %get-tuple-element.3), kind=kOutput, calls=%fused_computation.44 | convolution fusion | flops 679491072 | bytes 16516224 | tf_op jit(solution)/shard_map/tbj,bd->tdj/dot_general | solution.py:39
  132.5 2.0 copy.31
  134.5 0.0 reduce-scatter.3.cloned.1.call-update
  134.5 0.0 reduce-scatter.5.cloned.1.call-start
  134.6 2.3 copy.32
  136.9 12.4 %gather_fusion.2 = bf16[288,192,128]{2,1,0:T(8,128)(2,1)} fusion(bf16[192,48,128]{2,0,1:T(8,128)(2,1)S(1)} %bitcast.59, s32[1024]{0:T(1024)S(1)} %pad_clamp_fusion), kind=kCustom, calls=%fused_computation.2.clone | custom fusion | bytes 28312704 | tf_op jit(solution)/shard_map/jit(_take)/gather | solution.py:45
  149.4 20.0 %broadcast_multiply_fusion = f32[288,128,128]{2,1,0:T(8,128)} fusion(bf16[288,192,128]{2,1,0:T(8,128)(2,1)} %gather_fusion.2, pred[288]{0:T(512)(128)(4,1)S(1)} %get-tuple-element.9, bf16[288,192,128]{2,1,0:T(8,128)(2,1)} %gather_fusion, pred[288]{0:T(512)(128)(4,1)S(1)} %get-tuple-element.10), kind=kOutput, calls=%fused_computation.21 | convolution fusion | flops 1830813696 | bytes 47186496 | tf_op jit(solution)/shard_map/tbi,tbj->bij/dot_general | solution.py:49
  169.4 0.0 reduce-scatter.5.cloned.1.call-update
  169.4 0.0 reduce-scatter.3.cloned.1.call-done
  169.5 315.2 %reduce-scatter.5.cloned.1.call-done = f32[4608,128]{1,0:T(8,128)} async-done(((f32[36864,128]{1,0:T(8,128)}), f32[4608,128]{1,0:T(8,128)}) %reduce-scatter.5.cloned.1.call-update) | async-done | bytes 2359312 | tf_op jit(solution)/shard_map/reduce_scatter | solution.py:52
  (8 shorter events, 0.1 us)
Async XLA Ops:
  7.2 27.7 %all-gather.2.cloned.1.call-start = ((), (), s32[]{:S(2)}) async-start(), calls=%async_computation.2 | async-start | bytes 2949120 | tf_op jit(solution)/shard_map/all_gather | solution.py:15
  7.9 161.6 %reduce-scatter.3.cloned.1.call-start = ((), (), s32[]{:S(2)}) async-start(), calls=%async_computation.3 | async-start | bytes 2949120 | tf_op jit(solution)/shard_map/reduce_scatter | solution.py:42
  65.8 19.6 %copy-start = (bf16[192,6144]{1,0:T(8,128)(2,1)S(1)}, bf16[192,6144]{1,0:T(8,128)(2,1)}, u32[]{:S(2)}) copy-start(bf16[192,6144]{1,0:T(8,128)(2,1)} %param.8) | copy-start | bytes 7077892
  134.5 350.2 %reduce-scatter.5.cloned.1.call-start = ((), (), s32[]{:S(2)}) async-start(), calls=%async_computation.4 | async-start | bytes 21233664 | tf_op jit(solution)/shard_map/reduce_scatter | solution.py:52
Sparse Core Ops, SparseCore 0:
  9.6 25.2 all-gather.1
  134.6 33.0 reduce-scatter.2
  172.7 311.9 reduce-scatter.4
where the time goes:
time: 494 us; the launch traced here: 491 us
  waiting for transfers between devices  341 us (69%)
  matrix products  86.2 us (17%)
  local copies, waits for them, and re-layouts  45.9 us (9%)
  between operations  13.9 us (3%)
    reduce_scatter x1, waiting for transfers between devices, local(): lax.psum_scatter(local_grad.reshape(-1, block_size), 'dp', scatter_dimens...  315 us
    all_gather x1, waiting for transfers between devices, local(): full_grad = lax.all_gather(out_grad, 'blk', axis=1, tiled=True)  25.2 us
    dot_general x1, matrix products, local(): jnp.einsum('tbi,tbj->bij', act_panels, grad_panels, preferred_element_typ...  20 us
    dot_general x1, matrix products, local(): jnp.einsum('tbi,bf->tfi', down_terms, down_pick)  19.6 us
    dot_general x1, matrix products, local(): jnp.einsum('tbj,bij->tbi', grad_panels, w_down_blocks, preferred_element_...  16.5 us
    dot_general x1, matrix products, local(): jnp.einsum('tbi,bji->tbj', pre_panels, w_up_blocks, preferred_element_typ...  16.5 us
    dot_general x1, matrix products, local(): jnp.einsum('tbj,bd->tdj', up_terms, up_pick)  13.6 us
    gather x1, local copies, waits for them, and re-layouts, local(): jnp.take(pre_grad.reshape(tok_rows, hid_blocks, block_size), up_index[:,...  12.5 us
  transfers between devices with their start and end apart: 3, of which 2 were waited for; matrix products, arithmetic and copies ran while one was open for 7% of the time, Pallas kernels for 0%

commit v1 on v0

v1 whole, which is shorter than its diff:
```python
import functools

import jax
import jax.numpy as jnp
from jax import lax
from jax.experimental import pallas as pl
from jax.experimental.pallas import tpu as pltpu
from jax.sharding import PartitionSpec as P

inv_root_two = 0.7071067811865476
inv_root_twopi = 0.3989422804014327
MESH = pl.DeviceIdType.MESH
VMEM_BYTES = 58 << 20
DEEP, WIDE = 4, 2


def contract_last(a, b):
    return lax.dot_general(
        a, b, (((1,), (1,)), ((), ())), preferred_element_type=jnp.float32
    )


def chunk_of(count, most):
    return max(n for n in range(1, most + 1) if count % n == 0)


def hidden_kernel(
    per_step, group, down_ref, up_ref, grad_ref, slope_ref, wd_ref, wu_ref, out_ref,
    hid_acc, pre, feat_acc,
):
    phase, step = pl.program_id(0), pl.program_id(1)
    last = pl.num_programs(1) - 1

    @pl.when((phase == 0) & (step == 0))
    def _():
        hid_acc[...] = jnp.zeros_like(hid_acc)
        feat_acc[...] = jnp.zeros_like(feat_acc)

    @pl.when(phase == 0)
    def _():
        @pl.loop(0, per_step // group)
        def _(g):
            first = step * per_step + g * group
            terms = [
                contract_last(grad_ref[down_ref[first + i, 0]], wd_ref[g * group + i])
                for i in range(group)
            ]
            for i in range(group):
                hid_acc[down_ref[first + i, 1]] += terms[i]

    @pl.when((phase == 0) & (step == last))
    def _():
        @pl.loop(0, pre.shape[0])
        def _(c):
            pre[c] = (hid_acc[c] * slope_ref[c]).astype(pre.dtype)

    @pl.when(phase == 1)
    def _():
        @pl.loop(0, per_step // group)
        def _(g):
            first = step * per_step + g * group
            terms = [
                contract_last(pre[up_ref[first + i, 1]], wu_ref[g * group + i])
                for i in range(group)
            ]
            for i in range(group):
                feat_acc[up_ref[first + i, 0]] += terms[i]

    @pl.when((phase == 1) & (step == last))
    def _():
        @pl.loop(0, feat_acc.shape[0])
        def _(r):
            out_ref[r] = feat_acc[r].astype(out_ref.dtype)


def hidden_call(down_index, up_index, grads, slope, w_down, w_up):
    feats, rows, side = grads.shape
    hids = slope.shape[0]
    count = w_down.shape[0]
    per_step = chunk_of(count, 24)
    group = chunk_of(per_step, 8)
    steps = count // per_step
    whole = lambda shape: pl.BlockSpec(shape, lambda p, s, *_: (0, 0, 0))
    return pl.pallas_call(
        functools.partial(hidden_kernel, per_step, group),
        grid_spec=pltpu.PrefetchScalarGridSpec(
            num_scalar_prefetch=2,
            grid=(2, steps),
            in_specs=[
                whole(grads.shape),
                whole(slope.shape),
                pl.BlockSpec(
                    (per_step, side, side),
                    lambda p, s, *_: (jnp.where(p == 0, s, steps - 1), 0, 0),
                ),
                pl.BlockSpec(
                    (per_step, side, side),
                    lambda p, s, *_: (jnp.where(p == 0, 0, s), 0, 0),
                ),
            ],
            out_specs=whole(grads.shape),
            scratch_shapes=[
                pltpu.VMEM((hids, rows, side), jnp.float32),
                pltpu.VMEM((hids, rows, side), jnp.bfloat16),
                pltpu.VMEM((feats, rows, side), jnp.float32),
            ],
        ),
        out_shape=jax.ShapeDtypeStruct(grads.shape, jnp.bfloat16),
        compiler_params=pltpu.CompilerParams(vmem_limit_bytes=VMEM_BYTES),
        cost_estimate=pl.CostEstimate(
            flops=4 * count * rows * side * side,
            bytes_accessed=4 * count * side * side,
            transcendentals=0,
        ),
        name="hidden_grads",
    )(down_index, up_index, grads, slope, w_down, w_up)


def weight_kernel(
    chunks, ahead, scale, hid_ids, feat_ids, act_ref, grad_ref, out_ref,
    x_out, x_in, up_in, dn_in, z_out, acc,
    x_send, x_recv, up_recv, dn_recv, z_send,
):
    blk = lax.axis_index("blk")
    dp = lax.axis_index("dp")
    z, x = dp // WIDE, dp % WIDE
    per = out_ref.shape[0]
    n = per // chunks
    items = DEEP * chunks

    def at(zz, xx):
        return (zz * WIDE + xx, blk)

    barrier = pltpu.get_barrier_semaphore()
    pl.semaphore_signal(barrier, inc=1, device_id=at(z, 1 - x), device_id_type=MESH)

    @pl.when(z > 0)
    def _():
        pl.semaphore_signal(barrier, inc=1, device_id=at(z - 1, x), device_id_type=MESH)

    @pl.when(z < DEEP - 1)
    def _():
        pl.semaphore_signal(barrier, inc=1, device_id=at(z + 1, x), device_id_type=MESH)

    peers = 1 + (z > 0).astype(jnp.int32) + (z < DEEP - 1).astype(jnp.int32)
    pl.semaphore_wait(barrier, peers)

    def place(t):
        half, r = t // (2 * chunks), t % (2 * chunks)
        c, low = r // 2, r % 2
        return jnp.where(low == 0, DEEP - 1 - half, half), c

    def product(k):
        return jnp.dot(
            act_ref[hid_ids[k]], grad_ref[feat_ids[k]], preferred_element_type=jnp.float32
        )

    def x_copy(t):
        return pltpu.make_async_remote_copy(
            src_ref=x_out.at[t], dst_ref=x_in.at[t], send_sem=x_send.at[t],
            recv_sem=x_recv.at[t], device_id=at(z, 1 - x), device_id_type=MESH,
        )

    def up_copy(t):
        return pltpu.make_async_remote_copy(
            src_ref=z_out.at[t], dst_ref=up_in.at[t], send_sem=z_send.at[t],
            recv_sem=up_recv.at[t], device_id=at(z + 1, x), device_id_type=MESH,
        )

    def dn_copy(t):
        return pltpu.make_async_remote_copy(
            src_ref=z_out.at[t], dst_ref=dn_in.at[t], send_sem=z_send.at[t],
            recv_sem=dn_recv.at[t], device_id=at(z - 1, x), device_id_type=MESH,
        )

    def send_x(t):
        zt, c = place(t)
        base = (zt * WIDE + 1 - x) * per + c * n
        for i in range(n):
            x_out[t, i] = product(base + i).astype(x_out.dtype)
        x_copy(t).start()

    def handle(t):
        zt, c = place(t)
        base = (zt * WIDE + x) * per + c * n
        for i in range(n):
            acc[i] = product(base + i)
        x_copy(t).wait_recv()
        acc[...] += x_in[t].astype(jnp.float32)

        @pl.when((z <= zt) & (z > 0))
        def _():
            up_copy(t).wait_recv()
            acc[...] += up_in[t].astype(jnp.float32)

        @pl.when((z >= zt) & (z < DEEP - 1))
        def _():
            dn_copy(t).wait_recv()
            acc[...] += dn_in[t].astype(jnp.float32)

        @pl.when(z == zt)
        def _():
            out_ref[pl.ds(c * n, n)] = acc[...] * scale

        @pl.when(z < zt)
        def _():
            z_out[t] = acc[...].astype(z_out.dtype)
            up_copy(t).start()

        @pl.when(z > zt)
        def _():
            z_out[t] = acc[...].astype(z_out.dtype)
            dn_copy(t).start()

    @pl.loop(0, ahead)
    def _(t):
        send_x(t)

    @pl.loop(0, items + DEEP - 1)
    def _(u):
        @pl.when(u + ahead < items)
        def _():
            x_copy(u).wait_send()
            send_x(u + ahead)

        @pl.loop(0, DEEP)
        def _(lag):
            t = u - lag
            safe = jnp.clip(t, 0, items - 1)
            zt, _ = place(safe)
            late = jnp.where(
                z < zt, z, jnp.where(z > zt, DEEP - 1 - z, jnp.maximum(z, DEEP - 1 - z))
            )

            @pl.when((t >= 0) & (t < items) & (late == lag))
            def _():
                handle(safe)

    @pl.loop(items - ahead, items)
    def _(t):
        x_copy(t).wait_send()

    @pl.loop(0, items)
    def _(t):
        zt, _ = place(t)

        @pl.when(z != zt)
        def _():
            up_copy(t).wait_send()


def weight_call(hid_ids, feat_ids, acts, grads, scale):
    hids, side, rows = acts.shape
    count = hid_ids.shape[0]
    per = count // (DEEP * WIDE)
    chunks = chunk_of(per, 4)
    n = per // chunks
    items = DEEP * chunks
    ahead = min(3, items)
    slots = pltpu.VMEM((items, n, side, side), jnp.bfloat16)
    sems = pltpu.SemaphoreType.DMA((items,))
    return pl.pallas_call(
        functools.partial(weight_kernel, chunks, ahead, scale),
        out_shape=jax.ShapeDtypeStruct((per, side, side), jnp.float32),
        in_specs=[pl.BlockSpec(memory_space=pltpu.SMEM)] * 2
        + [pl.BlockSpec(memory_space=pltpu.VMEM)] * 2,
        out_specs=pl.BlockSpec(memory_space=pltpu.VMEM),
        scratch_shapes=[slots] * 5
        + [pltpu.VMEM((n, side, side), jnp.float32)]
        + [sems] * 5,
        compiler_params=pltpu.CompilerParams(
            collective_id=0, has_side_effects=True, vmem_limit_bytes=VMEM_BYTES
        ),
        cost_estimate=pl.CostEstimate(
            flops=2 * count * rows * side * side,
            bytes_accessed=4 * count * side * side,
            transcendentals=0,
        ),
        name="weight_grads",
    )(hid_ids, feat_ids, acts, grads)


def local(hidden_pre, out_grad, w_up_blocks, up_index, w_down_blocks, down_index):
    rows, hid_width = hidden_pre.shape
    side = w_up_blocks.shape[1]
    hids = hid_width // side
    count = w_down_blocks.shape[0]
    dp_size = lax.axis_size("dp")
    scale = float((rows * dp_size) ** (-0.5))
    own = out_grad.reshape(rows, -1, side).transpose(1, 0, 2)
    grads = lax.all_gather(own, "blk", axis=0, tiled=True)
    feats = grads.shape[0]
    pre_float = hidden_pre.astype(jnp.float32)
    normal_cdf = 0.5 * (1.0 + lax.erf(pre_float * inv_root_two))
    slope = normal_cdf + pre_float * jnp.exp(-0.5 * pre_float * pre_float) * inv_root_twopi
    slope = slope.reshape(rows, hids, side).transpose(1, 0, 2)
    acts = (pre_float * normal_cdf).astype(jnp.bfloat16)
    acts = acts.reshape(rows, hids, side).transpose(1, 2, 0)
    partial_sum = hidden_call(down_index, up_index, grads, slope, w_down_blocks, w_up_blocks)
    summed = lax.psum_scatter(partial_sum, "blk", scatter_dimension=0, tiled=True)
    summed = summed.transpose(1, 0, 2).reshape(rows, -1)
    if dp_size == DEEP * WIDE and count % dp_size == 0:
        weight_out = weight_call(down_index[:, 1], down_index[:, 0], acts, grads, scale)
        weight_out = weight_out.reshape(-1, side)
    else:
        local_grad = jnp.einsum(
            "bit,btj->bij",
            jnp.take(acts, down_index[:, 1], axis=0),
            jnp.take(grads, down_index[:, 0], axis=0),
            preferred_element_type=jnp.float32,
        )
        weight_out = lax.psum_scatter(
            (local_grad * scale).reshape(-1, side), "dp", scatter_dimension=0, tiled=True
        )
    return (summed, weight_out)


def solution(mesh):
    placed = (
        P("dp", "blk"),
        P("dp", "blk"),
        P("blk", None, None),
        P("blk", None),
        P("blk", None, None),
        P("blk", None),
    )
    return jax.shard_map(
        local,
        mesh=mesh,
        in_specs=placed,
        out_specs=(P("dp", "blk"), P(("blk", "dp"), None)),
        check_vma=False,
    )
```

time: 494 us -> 215 us (0.44)
  waiting for transfers between devices: 341 us -> 17.4 us
  Pallas kernels: 0 us -> 163 us
  matrix products: 86.2 us -> 0 us
  local copies, waits for them, and re-layouts: 45.9 us -> 15.5 us
    reduce_scatter x2 -> x1, waiting for transfers between devices: 315 us -> 0.02 us  [local(): lax.psum_scatter(partial_sum, 'blk', scatter_dimension=0, tiled=True)]
    pallas_call x0 -> x2, Pallas kernels: none -> 163 us  [the longest x1 126 us: weight_call(): pl.pallas_call(functools.partial(weight_kernel, chunks, ahead, scale), ou...]
    dot_general x5 -> x0, matrix products: 86.2 us -> none  [the longest x1 20 us: local(): jnp.einsum('tbi,tbj->bij', act_panels, grad_panels, preferred_element_typ...]
    gather x3 -> x0, local copies, waits for them, and re-layouts: 37.1 us -> none  [the longest x1 12.5 us: local(): jnp.take(pre_grad.reshape(tok_rows, hid_blocks, block_size), up_index[:,...]
    all_gather x1, waiting for transfers between devices: 25.2 us -> 17.4 us  [local(): grads = lax.all_gather(own, 'blk', axis=0, tiled=True)]
  transfers between devices with their start and end apart: 3 -> 2, of which waited for: 2 -> 1; matrix products, arithmetic and copies ran while one was open for 7% -> 5% of each run, Pallas kernels for 0% -> 59%
where the time goes in v1:
time: 215 us; the launch traced here: 214 us
  Pallas kernels  163 us (76%)
  waiting for transfers between devices  17.4 us (8%)
  local copies, waits for them, and re-layouts  15.5 us (7%)
  between operations  14.1 us (7%)
  other arithmetic  3.77 us (2%)
    pallas_call x1, Pallas kernels, weight_call(): pl.pallas_call(functools.partial(weight_kernel, chunks, ahead, scale), ou...  126 us
    pallas_call x1, Pallas kernels, hidden_call(): pl.pallas_call(functools.partial(hidden_kernel, per_step, group), grid_sp...  37.5 us
    all_gather x1, waiting for transfers between devices, local(): grads = lax.all_gather(own, 'blk', axis=0, tiled=True)  17.4 us
    unnamed x7, local copies, waits for them, and re-layouts  4.85 us
  transfers between devices with their start and end apart: 2, of which 1 were waited for; matrix products, arithmetic and copies ran while one was open for 5% of the time, Pallas kernels for 59%

profile of v1, /device:TPU:8, one launch (start us, length us, event | category | flops | bytes accessed | tf_op | source)
XLA Modules:
  0.0 214.1 jit_solution(15505386032681706269)
XLA Ops:
  7.2 0.0 all-gather.2.cloned.1.call-start
  7.2 1.5 reshape.19
  8.7 1.0 copy.17
  9.7 0.0 all-gather.2.cloned.1.call-update
  9.7 0.0 reduce-scatter.2.cloned.1.call-start
  9.8 3.8 %fusion.7 = (bf16[192,6144]{1,0:T(8,128)(2,1)S(1)}, f32[24,48,8,128]{3,2,1,0:T(8,128)S(1)}) fusion(bf16[192,6144]{1,0:T(8,128)(2,1)} %param.6), kind=kLoop, calls=%fused_computation.12 | loop fusion | flops 12976128 | bytes 9437184 | tf_op jit(solution)/shard_map/convert_element_type | solution.py:297
  13.5 0.0 copy-start
  13.5 0.0 copy-start.1
  13.6 2.8 %copy.27 = f32[24,48,8,128]{3,2,0,1:T(8,128)} copy(f32[24,48,8,128]{3,2,1,0:T(8,128)S(1)} %get-tuple-element.5) | data formatting | bytes 9437184 | tf_op jit(solution)/shard_map/reshape | solution.py:296
  16.4 0.0 copy-done
  16.4 0.8 copy.19.down_ref
  17.2 0.0 copy-done.1
  17.2 0.8 copy.20.up_ref
  18.0 17.4 %all-gather.2.cloned.1.call-done.grad_ref = bf16[48,192,128]{2,1,0:T(8,128)(2,1)} async-done(((bf16[12,192,128]{2,1,0:T(8,128)(2,1)}), bf16[48,192,128]{2,1,0:T(8,128)(2,1)}) %all-gather.2.cloned.1.call-update) | async-done | bytes 2359312 | tf_op jit(solution)/shard_map/all_gather | solution.py:291
  35.4 37.5 %hidden_grads.1 = bf16[48,192,128]{2,1,0:T(8,128)(2,1)} custom-call(s32[288,2]{1,0:T(8,128)} %copy.19.down_ref, s32[288,2]{1,0:T(8,128)} %copy.20.up_ref, bf16[48,192,128]{2,1,0:T(8,128)(2,1)} %all-gather.2.cloned.1.call-done.grad_ref, f32[48,192,128]{2,1,0:T(8,128)} %bitcast.19, bf16[288,128,128]{2,1,0:T(8,128)(2,1)} %wd_ref.1, bf16[288,128,128]{2,1,0:T(8,128)(2,1)} %wu_ref.1), custom_call_target="tpu_custom_call" | custom-call | flops 3623878656 | bytes 18874368 | tf_op jit(solution)/shard_map/hidden_grads/pallas_call | solution.py:84
  72.9 0.0 reduce-scatter.2.cloned.1.call-update
  73.0 2.8 %copy.22 = bf16[192,6144]{0,1:T(8,128)(2,1)} copy(bf16[192,6144]{1,0:T(8,128)(2,1)S(1)} %get-tuple-element.4) | data formatting | bytes 4718592 | tf_op jit(solution)/shard_map/convert_element_type | solution.py:297
  75.8 0.6 slice_reduce_fusion
  76.4 125.6 %weight_grads.1 = f32[36,128,128]{2,1,0:T(8,128)} custom-call(s32[288]{0:T(512)} %get-tuple-element.3.hid_ids, s32[288]{0:T(512)} %get-tuple-element.2.feat_ids, bf16[48,128,192]{2,1,0:T(8,128)(2,1)} %bitcast.20, bf16[48,192,128]{2,1,0:T(8,128)(2,1)} %all-gather.2.cloned.1.call-done.grad_ref), custom_call_target="tpu_custom_call" | custom-call | flops 1811939328 | bytes 18874368 | tf_op jit(solution)/shard_map/weight_grads/pallas_call | solution.py:262
  202.0 0.0 reduce-scatter.2.cloned.1.call-done
  202.0 1.9 copy_bitcast_fusion
  204.0 3.2 %copy.29 = f32[4608,128]{1,0:T(8,128)} copy(f32[4608,128]{1,0:T(8,128)} %bitcast.21) | data formatting | bytes 4718592
Async XLA Ops:
  7.2 28.2 %all-gather.2.cloned.1.call-start = ((), (), s32[]{:S(2)}) async-start(), calls=%async_computation.1 | async-start | bytes 2949120 | tf_op jit(solution)/shard_map/all_gather | solution.py:291
  9.7 192.3 %reduce-scatter.2.cloned.1.call-start = ((), (), s32[]{:S(2)}) async-start(), calls=%async_computation.2 | async-start | bytes 2949120 | tf_op jit(solution)/shard_map/reduce_scatter | solution.py:300
  13.5 2.9 %copy-start = (s32[288,2]{0,1:T(2,128)S(1)}, s32[288,2]{0,1:T(2,128)}, u32[]{:S(2)}) copy-start(s32[288,2]{0,1:T(2,128)} %param.11) | copy-start | bytes 6916
  13.5 3.7 %copy-start.1 = (s32[288,2]{0,1:T(2,128)S(1)}, s32[288,2]{0,1:T(2,128)}, u32[]{:S(2)}) copy-start(s32[288,2]{0,1:T(2,128)} %param.9) | copy-start | bytes 6916
Sparse Core Ops, SparseCore 0:
  10.1 25.2 all-gather.1
  73.1 33.0 reduce-scatter.1

commit v2 on v1

--- a/solution.py
+++ b/solution.py
@@ -116,9 +116,31 @@
     )(down_index, up_index, grads, slope, w_down, w_up)
 
 
+def item_place(chunks, t):
+    half, r = t // (2 * chunks), t % (2 * chunks)
+    c, low = r // 2, r % 2
+    return jnp.where(low == 0, DEEP - 1 - half, half), c
+
+
+def early_kernel(chunks, per, hid_ids, feat_ids, act_ref, grad_ref, out_ref):
+    x = lax.axis_index("dp") % WIDE
+    n = per // chunks
+
+    @pl.loop(0, out_ref.shape[0])
+    def _(t):
+        zt, c = item_place(chunks, t)
+        base = (zt * WIDE + 1 - x) * per + c * n
+        for i in range(n):
+            out_ref[t, i] = jnp.dot(
+                act_ref[hid_ids[base + i]],
+                grad_ref[feat_ids[base + i]],
+                preferred_element_type=jnp.float32,
+            ).astype(out_ref.dtype)
+
+
 def weight_kernel(
-    chunks, ahead, scale, hid_ids, feat_ids, act_ref, grad_ref, out_ref,
-    x_out, x_in, up_in, dn_in, z_out, acc,
+    chunks, early, ahead, scale, hid_ids, feat_ids, act_ref, grad_ref, early_ref,
+    out_ref, x_out, x_in, up_in, dn_in, z_out, acc,
     x_send, x_recv, up_recv, dn_recv, z_send,
 ):
     blk = lax.axis_index("blk")
@@ -146,9 +168,7 @@
     pl.semaphore_wait(barrier, peers)
 
     def place(t):
-        half, r = t // (2 * chunks), t % (2 * chunks)
-        c, low = r // 2, r % 2
-        return jnp.where(low == 0, DEEP - 1 - half, half), c
+        return item_place(chunks, t)
 
     def product(k):
         return jnp.dot(
@@ -157,8 +177,9 @@
 
     def x_copy(t):
         return pltpu.make_async_remote_copy(
-            src_ref=x_out.at[t], dst_ref=x_in.at[t], send_sem=x_send.at[t],
-            recv_sem=x_recv.at[t], device_id=at(z, 1 - x), device_id_type=MESH,
+            src_ref=x_out.at[t - early], dst_ref=x_in.at[t - early],
+            send_sem=x_send.at[t - early], recv_sem=x_recv.at[t - early],
+            device_id=at(z, 1 - x), device_id_type=MESH,
         )
 
     def up_copy(t):
@@ -177,7 +198,7 @@
         zt, c = place(t)
         base = (zt * WIDE + 1 - x) * per + c * n
         for i in range(n):
-            x_out[t, i] = product(base + i).astype(x_out.dtype)
+            x_out[t - early, i] = product(base + i).astype(x_out.dtype)
         x_copy(t).start()
 
     def handle(t):
@@ -185,8 +206,15 @@
         base = (zt * WIDE + x) * per + c * n
         for i in range(n):
             acc[i] = product(base + i)
-        x_copy(t).wait_recv()
-        acc[...] += x_in[t].astype(jnp.float32)
+
+        @pl.when(t < early)
+        def _():
+            acc[...] += early_ref[jnp.minimum(t, early - 1)].astype(jnp.float32)
+
+        @pl.when(t >= early)
+        def _():
+            x_copy(t).wait_recv()
+            acc[...] += x_in[t - early].astype(jnp.float32)
 
         @pl.when((z <= zt) & (z > 0))
         def _():
@@ -212,16 +240,18 @@
             z_out[t] = acc[...].astype(z_out.dtype)
             dn_copy(t).start()
 
-    @pl.loop(0, ahead)
+    @pl.loop(early, early + ahead)
     def _(t):
         send_x(t)
 
     @pl.loop(0, items + DEEP - 1)
     def _(u):
-        @pl.when(u + ahead < items)
-        def _():
-            x_copy(u).wait_send()
-            send_x(u + ahead)
+        later = early + ahead + u // 2 - 1
+
+        @pl.when((u % 2 == 0) & (u > 0) & (later < items))
+        def _():
+            x_copy(later - ahead).wait_send()
+            send_x(later)
 
         @pl.loop(0, DEEP)
         def _(lag):
@@ -250,34 +280,131 @@
 
 
 def weight_call(hid_ids, feat_ids, acts, grads, scale):
-    hids, side, rows = acts.shape
+    side, rows = acts.shape[1:]
     count = hid_ids.shape[0]
     per = count // (DEEP * WIDE)
-    chunks = chunk_of(per, 4)
+    chunks = chunk_of(per, 6)
     n = per // chunks
     items = DEEP * chunks
-    ahead = min(3, items)
-    slots = pltpu.VMEM((items, n, side, side), jnp.bfloat16)
-    sems = pltpu.SemaphoreType.DMA((items,))
+    early = items * 3 // 8
+    late = items - early
+    ahead = late // 2
+    smem, vmem = (pl.BlockSpec(memory_space=m) for m in (pltpu.SMEM, pltpu.VMEM))
+    cost = lambda share: pl.CostEstimate(
+        flops=2 * int(count * share) * rows * side * side,
+        bytes_accessed=4 * count * side * side,
+        transcendentals=0,
+    )
+    first = pl.pallas_call(
+        functools.partial(early_kernel, chunks, per),
+        out_shape=jax.ShapeDtypeStruct((early, n, side, side), jnp.bfloat16),
+        in_specs=[smem] * 2 + [vmem] * 2,
+        out_specs=vmem,
+        compiler_params=pltpu.CompilerParams(vmem_limit_bytes=VMEM_BYTES),
+        cost_estimate=cost(0.2),
+        name="early_grads",
+    )(hid_ids, feat_ids, acts, grads)
+    first = lax.ppermute(first, "dp", [(d, d ^ 1) for d in range(DEEP * WIDE)])
+    slot = lambda k: pltpu.VMEM((k, n, side, side), jnp.bfloat16)
+    sems = lambda k: pltpu.SemaphoreType.DMA((k,))
     return pl.pallas_call(
-        functools.partial(weight_kernel, chunks, ahead, scale),
+        functools.partial(weight_kernel, chunks, early, ahead, scale),
         out_shape=jax.ShapeDtypeStruct((per, side, side), jnp.float32),
-        in_specs=[pl.BlockSpec(memory_space=pltpu.SMEM)] * 2
-        + [pl.BlockSpec(memory_space=pltpu.VMEM)] * 2,
-        out_specs=pl.BlockSpec(memory_space=pltpu.VMEM),
-        scratch_shapes=[slots] * 5
+        in_specs=[smem] * 2 + [vmem] * 3,
+        out_specs=vmem,
+        scratch_shapes=[slot(late)] * 2
+        + [slot(items)] * 3
         + [pltpu.VMEM((n, side, side), jnp.float32)]
-        + [sems] * 5,
+        + [sems(late)] * 2
+        + [sems(items)] * 3,
         compiler_params=pltpu.CompilerParams(
             collective_id=0, has_side_effects=True, vmem_limit_bytes=VMEM_BYTES
         ),
+        cost_estimate=cost(0.8),
+        name="weight_grads",
+    )(hid_ids, feat_ids, acts, grads, first)
+
+
+def gelu_parts(pre):
+    normal_cdf = 0.5 * (1.0 + lax.erf(pre * inv_root_two))
+    slope = normal_cdf + pre * jnp.exp(-0.5 * pre * pre) * inv_root_twopi
+    return (pre * normal_cdf).astype(jnp.bfloat16), slope
+
+
+def gather_kernel(
+    parts, hid_ref, own_ref, grad_ref, slope_ref, act_ref,
+    y_send, y_recv, c_send, c_recv, f_send, f_recv,
+):
+    dp, blk = lax.axis_index("dp"), lax.axis_index("blk")
+    core, y = blk % 2, blk // 2
+    beside, across = y * 2 + 1 - core, (1 - y) * 2 + core
+    side = grad_ref.shape[2]
+    feats = own_ref.shape[1] // side
+    hids = act_ref.shape[0]
+    n, h = feats // parts, hids // parts
+
+    barrier = pltpu.get_barrier_semaphore()
+    for peer in (beside, across):
+        pl.semaphore_signal(barrier, inc=1, device_id=(dp, peer), device_id_type=MESH)
+    for f in range(feats):
+        grad_ref[blk * feats + f] = own_ref[:, f * side : (f + 1) * side]
+    pl.semaphore_wait(barrier, 2)
+
+    def copy(origin, q, target, send, recv):
+        place = grad_ref.at[pl.ds(origin * feats + q * n, n)]
+        return pltpu.make_async_remote_copy(
+            src_ref=place, dst_ref=place, send_sem=send.at[q], recv_sem=recv.at[q],
+            device_id=(dp, target), device_id_type=MESH,
+        )
+
+    for q in range(parts):
+        copy(blk, q, across, y_send, y_recv).start()
+    for q in range(parts):
+        copy(blk, q, beside, c_send, c_recv).start()
+    for q in range(parts):
+
+        @pl.loop(q * h, (q + 1) * h)
+        def _(c):
+            pre = hid_ref[:, pl.ds(pl.multiple_of(c * side, side), side)]
+            act, slope = gelu_parts(pre.astype(jnp.float32))
+            slope_ref[c] = slope
+            act_ref[c] = act.T
+
+        copy(across, q, across, y_send, y_recv).wait_recv()
+        copy(across, q, beside, f_send, f_recv).start()
+    for q in range(parts):
+        copy(blk, q, across, y_send, y_recv).wait_send()
+        copy(blk, q, beside, c_send, c_recv).wait_send()
+        copy(beside, q, beside, c_send, c_recv).wait_recv()
+        copy(across, q, beside, f_send, f_recv).wait_send()
+        copy(beside ^ 2, q, beside, f_send, f_recv).wait_recv()
+
+
+def gather_call(hidden_pre, out_grad, side, feats):
+    rows, hid_width = hidden_pre.shape
+    hids = hid_width // side
+    parts = next(n for n in (4, 2, 1) if feats // 4 % n == 0 and hids % n == 0)
+    vmem = pl.BlockSpec(memory_space=pltpu.VMEM)
+    return pl.pallas_call(
+        functools.partial(gather_kernel, parts),
+        out_shape=(
+            jax.ShapeDtypeStruct((feats, rows, side), jnp.bfloat16),
+            jax.ShapeDtypeStruct((hids, rows, side), jnp.float32),
+            jax.ShapeDtypeStruct((hids, side, rows), jnp.bfloat16),
+        ),
+        in_specs=[vmem] * 2,
+        out_specs=(vmem,) * 3,
+        scratch_shapes=[pltpu.SemaphoreType.DMA((parts,))] * 6,
+        compiler_params=pltpu.CompilerParams(
+            collective_id=1, has_side_effects=True, vmem_limit_bytes=VMEM_BYTES
+        ),
         cost_estimate=pl.CostEstimate(
-            flops=2 * count * rows * side * side,
-            bytes_accessed=4 * count * side * side,
-            transcendentals=0,
-        ),
-        name="weight_grads",
-    )(hid_ids, feat_ids, acts, grads)
+            flops=40 * rows * hid_width,
+            bytes_accessed=8 * rows * hid_width,
+            transcendentals=2 * rows * hid_width,
+        ),
+        name="gather_gelu",
+    )(hidden_pre, out_grad)
 
 
 def local(hidden_pre, out_grad, w_up_blocks, up_index, w_down_blocks, down_index):
@@ -287,15 +414,15 @@
     count = w_down_blocks.shape[0]
     dp_size = lax.axis_size("dp")
     scale = float((rows * dp_size) ** (-0.5))
-    own = out_grad.reshape(rows, -1, side).transpose(1, 0, 2)
-    grads = lax.all_gather(own, "blk", axis=0, tiled=True)
-    feats = grads.shape[0]
-    pre_float = hidden_pre.astype(jnp.float32)
-    normal_cdf = 0.5 * (1.0 + lax.erf(pre_float * inv_root_two))
-    slope = normal_cdf + pre_float * jnp.exp(-0.5 * pre_float * pre_float) * inv_root_twopi
-    slope = slope.reshape(rows, hids, side).transpose(1, 0, 2)
-    acts = (pre_float * normal_cdf).astype(jnp.bfloat16)
-    acts = acts.reshape(rows, hids, side).transpose(1, 2, 0)
+    if lax.axis_size("blk") == 4:
+        feats = 4 * out_grad.shape[1] // side
+        grads, slope, acts = gather_call(hidden_pre, out_grad, side, feats)
+    else:
+        own = out_grad.reshape(rows, -1, side).transpose(1, 0, 2)
+        grads = lax.all_gather(own, "blk", axis=0, tiled=True)
+        acts, slope = gelu_parts(hidden_pre.astype(jnp.float32))
+        slope = slope.reshape(rows, hids, side).transpose(1, 0, 2)
+        acts = acts.reshape(rows, hids, side).transpose(1, 2, 0)
     partial_sum = hidden_call(down_index, up_index, grads, slope, w_down_blocks, w_up_blocks)
     summed = lax.psum_scatter(partial_sum, "blk", scatter_dimension=0, tiled=True)
     summed = summed.transpose(1, 0, 2).reshape(rows, -1)

time: 215 us -> 241 us (1.12)
  waiting for transfers between devices: 17.4 us -> 39.6 us
  Pallas kernels: 163 us -> 174 us
  local copies, waits for them, and re-layouts: 15.5 us -> 10.6 us
  other arithmetic: 3.77 us -> 0 us
    ppermute x0 -> x1, waiting for transfers between devices: none -> 39.6 us  [weight_call(): first = lax.ppermute(first, 'dp', [(d, d ^ 1) for d in range(DEEP * WIDE)])]
    all_gather x1 -> x0, waiting for transfers between devices: 17.4 us -> none  [local(): grads = lax.all_gather(own, 'blk', axis=0, tiled=True)]
    pallas_call x1 -> x3, Pallas kernels: 126 us -> 137 us  [the longest x1 108 us: weight_call(): pl.pallas_call(functools.partial(weight_kernel, chunks, early, ahead, sca...]
    reshape x2 -> x0, local copies, waits for them, and re-layouts: 4.34 us -> none  [the longest x1 2.83 us: local(): slope = slope.reshape(rows, hids, side).transpose(1, 0, 2)]
    convert_element_type x1 -> x0, other arithmetic: 3.77 us -> none  [local(): acts = (pre_float * normal_cdf).astype(jnp.bfloat16)]
    unnamed x7, local copies, waits for them, and re-layouts: 4.85 us -> 8.05 us
    convert_element_type x1 -> x0, local copies, waits for them, and re-layouts: 2.82 us -> none  [local(): acts = (pre_float * normal_cdf).astype(jnp.bfloat16)]
  transfers between devices with their start and end apart: 2 -> 2, of which waited for: 1 -> 1; matrix products, arithmetic and copies ran while one was open for 5% -> 0% of each run, Pallas kernels for 59% -> 48%
where the time goes in v2:
time: 241 us; the launch traced here: 240 us
  Pallas kernels  174 us (72%)
  waiting for transfers between devices  39.6 us (16%)
  between operations  14.1 us (6%)
  local copies, waits for them, and re-layouts  10.6 us (4%)
    pallas_call x1, Pallas kernels, weight_call(): pl.pallas_call(functools.partial(weight_kernel, chunks, early, ahead, sca...  108 us
    ppermute x1, waiting for transfers between devices, weight_call(): first = lax.ppermute(first, 'dp', [(d, d ^ 1) for d in range(DEEP * WIDE)])  39.6 us
    pallas_call x1, Pallas kernels, hidden_call(): pl.pallas_call(functools.partial(hidden_kernel, per_step, group), grid_sp...  37.5 us
    pallas_call x1, Pallas kernels, gather_call(): pl.pallas_call(functools.partial(gather_kernel, parts), out_shape=(jax.Sh...  22.4 us
    unnamed x7, local copies, waits for them, and re-layouts  8.05 us
    pallas_call x1, Pallas kernels, weight_call(): pl.pallas_call(functools.partial(early_kernel, chunks, per), out_shape=ja...  6.36 us
  transfers between devices with their start and end apart: 2, of which 1 were waited for; matrix products, arithmetic and copies ran while one was open for 0% of the time, Pallas kernels for 48%

profile of v2, /device:TPU:8, one launch (start us, length us, event | category | flops | bytes accessed | tf_op | source)
XLA Modules:
  0.0 239.9 jit_solution(11075844303440950342)
XLA Ops:
  7.2 0.0 reduce-scatter.2.cloned.1.call-start
  7.2 1.5 copy.10.down_ref
  8.7 1.5 copy.11.up_ref
  10.2 22.4 %gather_gelu.1 = (bf16[48,192,128]{2,1,0:T(8,128)(2,1)}, f32[48,192,128]{2,1,0:T(8,128)}, bf16[48,128,192]{2,1,0:T(8,128)(2,1)}) custom-call(bf16[192,6144]{1,0:T(8,128)(2,1)} %hid_ref.1, bf16[192,1536]{1,0:T(8,128)(2,1)} %own_ref.1), custom_call_target="tpu_custom_call" | custom-call | flops 47185920 | bytes 9437184 | tf_op jit(solution)/shard_map/gather_gelu/pallas_call | solution.py:388
  32.6 37.5 %hidden_grads.1 = bf16[48,192,128]{2,1,0:T(8,128)(2,1)} custom-call(s32[288,2]{1,0:T(8,128)} %copy.10.down_ref, s32[288,2]{1,0:T(8,128)} %copy.11.up_ref, bf16[48,192,128]{2,1,0:T(8,128)(2,1)} %get-tuple-element.5.grad_ref, f32[48,192,128]{2,1,0:T(8,128)} %get-tuple-element.6.slope_ref, bf16[288,128,128]{2,1,0:T(8,128)(2,1)} %wd_ref.1, ...), custom_call_target="tpu_custom_call" | custom-call | flops 3623878656 | bytes 18874368 | tf_op jit(solution)/shard_map/hidden_grads/pallas_call | solution.py:84
  70.1 0.0 copy-start.1
  70.1 0.0 reduce-scatter.2.cloned.1.call-update
  70.2 0.7 copy-done.1
  70.8 0.6 slice_reduce_fusion
  71.4 6.4 %early_grads.1 = bf16[9,6,128,128]{3,2,1,0:T(8,128)(2,1)} custom-call(s32[288]{0:T(512)} %get-tuple-element.9.hid_ids, s32[288]{0:T(512)} %get-tuple-element.8.feat_ids, bf16[48,128,192]{2,1,0:T(8,128)(2,1)} %get-tuple-element.7.act_ref, bf16[48,192,128]{2,1,0:T(8,128)(2,1)} %get-tuple-element.5.grad_ref), custom_call_target="tpu_custom_call" | custom-call | flops 358612992 | bytes 18874368 | tf_op jit(solution)/shard_map/early_grads/pallas_call | solution.py:298
  77.8 1.5 collective-permute-start
  79.3 39.6 %collective-permute-done.early_ref = bf16[9,6,128,128]{3,2,1,0:T(8,128)(2,1)S(1)} collective-permute-done((bf16[9,6,128,128]{3,2,1,0:T(8,128)(2,1)}, bf16[9,6,128,128]{3,2,1,0:T(8,128)(2,1)S(1)}, u32[]{:S(2)}, u32[]{:S(2)}) %collective-permute-start) | collective-permute-done | bytes 1769504 | tf_op jit(solution)/shard_map/ppermute | solution.py:307
  118.9 0.0 copy-start
  118.9 1.2 copy-done
  120.1 107.8 %weight_grads.1 = f32[36,128,128]{2,1,0:T(8,128)} custom-call(s32[288]{0:T(512)} %get-tuple-element.9.hid_ids, s32[288]{0:T(512)} %get-tuple-element.8.feat_ids, bf16[48,128,192]{2,1,0:T(8,128)(2,1)} %get-tuple-element.7.act_ref, bf16[48,192,128]{2,1,0:T(8,128)(2,1)} %get-tuple-element.5.grad_ref, bf16[9,6,128,128]{3,2,1,0:T(8,128)(2,1)} %copy-done), custom_call_target="tpu_custom_call" | custom-call | flops 1447034880 | bytes 18874368 | tf_op jit(solution)/shard_map/weight_grads/pallas_call | solution.py:310
  227.9 0.0 reduce-scatter.2.cloned.1.call-done
  227.9 1.9 copy_bitcast_fusion
  229.9 3.2 %copy.16 = f32[4608,128]{1,0:T(8,128)} copy(f32[4608,128]{1,0:T(8,128)} %bitcast.7) | data formatting | bytes 4718592
Async XLA Ops:
  7.2 220.7 %reduce-scatter.2.cloned.1.call-start = ((), (), s32[]{:S(2)}) async-start(), calls=%async_computation.1 | async-start | bytes 2949120 | tf_op jit(solution)/shard_map/reduce_scatter | solution.py:427
  70.1 0.7 copy-start.1
  77.8 41.1 %collective-permute-start = (bf16[9,6,128,128]{3,2,1,0:T(8,128)(2,1)}, bf16[9,6,128,128]{3,2,1,0:T(8,128)(2,1)S(1)}, u32[]{:S(2)}, u32[]{:S(2)}) collective-permute-start(bf16[9,6,128,128]{3,2,1,0:T(8,128)(2,1)} %early_grads.1), channel_id=1, source_target_pairs={{0,4},{4,0},{8,12},{12,8},{16,20},{20,16},{24,28},{28,24},{1,5},{5... | collective-permute-start | bytes 5308424 | tf_op jit(solution)/shard_map/ppermute | solution.py:307
  118.9 1.2 copy-start
Sparse Core Ops, SparseCore 0:
  70.3 33.8 reduce-scatter.1

commit v3 on v1

--- a/solution.py
+++ b/solution.py
@@ -41,12 +41,10 @@
         @pl.loop(0, per_step // group)
         def _(g):
             first = step * per_step + g * group
-            terms = [
-                contract_last(grad_ref[down_ref[first + i, 0]], wd_ref[g * group + i])
-                for i in range(group)
-            ]
             for i in range(group):
-                hid_acc[down_ref[first + i, 1]] += terms[i]
+                hid_acc[down_ref[first + i, 1]] += contract_last(
+                    grad_ref[down_ref[first + i, 0]], wd_ref[g * group + i]
+                )
 
     @pl.when((phase == 0) & (step == last))
     def _():
@@ -59,12 +57,10 @@
         @pl.loop(0, per_step // group)
         def _(g):
             first = step * per_step + g * group
-            terms = [
-                contract_last(pre[up_ref[first + i, 1]], wu_ref[g * group + i])
-                for i in range(group)
-            ]
             for i in range(group):
-                feat_acc[up_ref[first + i, 0]] += terms[i]
+                feat_acc[up_ref[first + i, 0]] += contract_last(
+                    pre[up_ref[first + i, 1]], wu_ref[g * group + i]
+                )
 
     @pl.when((phase == 1) & (step == last))
     def _():
@@ -78,7 +74,7 @@
     hids = slope.shape[0]
     count = w_down.shape[0]
     per_step = chunk_of(count, 24)
-    group = chunk_of(per_step, 8)
+    group = chunk_of(per_step, 12)
     steps = count // per_step
     whole = lambda shape: pl.BlockSpec(shape, lambda p, s, *_: (0, 0, 0))
     return pl.pallas_call(
@@ -253,10 +249,10 @@
     hids, side, rows = acts.shape
     count = hid_ids.shape[0]
     per = count // (DEEP * WIDE)
-    chunks = chunk_of(per, 4)
+    chunks = chunk_of(per, 6)
     n = per // chunks
     items = DEEP * chunks
-    ahead = min(3, items)
+    ahead = min(5, items)
     slots = pltpu.VMEM((items, n, side, side), jnp.bfloat16)
     sems = pltpu.SemaphoreType.DMA((items,))
     return pl.pallas_call(
@@ -280,6 +276,88 @@
     )(hid_ids, feat_ids, acts, grads)
 
 
+def gelu_parts(pre):
+    normal_cdf = 0.5 * (1.0 + lax.erf(pre * inv_root_two))
+    slope = normal_cdf + pre * jnp.exp(-0.5 * pre * pre) * inv_root_twopi
+    return (pre * normal_cdf).astype(jnp.bfloat16), slope
+
+
+def gather_kernel(
+    parts, hid_ref, own_ref, grad_ref, slope_ref, act_ref,
+    y_send, y_recv, c_send, c_recv, f_send, f_recv,
+):
+    dp, blk = lax.axis_index("dp"), lax.axis_index("blk")
+    core, y = blk % 2, blk // 2
+    beside, across = y * 2 + 1 - core, (1 - y) * 2 + core
+    side = grad_ref.shape[2]
+    feats = own_ref.shape[1] // side
+    hids = act_ref.shape[0]
+    n, h = feats // parts, hids // parts
+
+    barrier = pltpu.get_barrier_semaphore()
+    for peer in (beside, across):
+        pl.semaphore_signal(barrier, inc=1, device_id=(dp, peer), device_id_type=MESH)
+    for f in range(feats):
+        grad_ref[blk * feats + f] = own_ref[:, f * side : (f + 1) * side]
+    pl.semaphore_wait(barrier, 2)
+
+    def copy(origin, q, target, send, recv):
+        place = grad_ref.at[pl.ds(origin * feats + q * n, n)]
+        return pltpu.make_async_remote_copy(
+            src_ref=place, dst_ref=place, send_sem=send.at[q], recv_sem=recv.at[q],
+            device_id=(dp, target), device_id_type=MESH,
+        )
+
+    for q in range(parts):
+        copy(blk, q, across, y_send, y_recv).start()
+    for q in range(parts):
+        copy(blk, q, beside, c_send, c_recv).start()
+    for q in range(parts):
+
+        @pl.loop(q * h, (q + 1) * h)
+        def _(c):
+            pre = hid_ref[:, pl.ds(pl.multiple_of(c * side, side), side)]
+            act, slope = gelu_parts(pre.astype(jnp.float32))
+            slope_ref[c] = slope
+            act_ref[c] = act.T
+
+        copy(across, q, across, y_send, y_recv).wait_recv()
+        copy(across, q, beside, f_send, f_recv).start()
+    for q in range(parts):
+        copy(blk, q, across, y_send, y_recv).wait_send()
+        copy(blk, q, beside, c_send, c_recv).wait_send()
+        copy(beside, q, beside, c_send, c_recv).wait_recv()
+        copy(across, q, beside, f_send, f_recv).wait_send()
+        copy(beside ^ 2, q, beside, f_send, f_recv).wait_recv()
+
+
+def gather_call(hidden_pre, out_grad, side, feats):
+    rows, hid_width = hidden_pre.shape
+    hids = hid_width // side
+    parts = next(n for n in (4, 2, 1) if feats // 4 % n == 0 and hids % n == 0)
+    vmem = pl.BlockSpec(memory_space=pltpu.VMEM)
+    return pl.pallas_call(
+        functools.partial(gather_kernel, parts),
+        out_shape=(
+            jax.ShapeDtypeStruct((feats, rows, side), jnp.bfloat16),
+            jax.ShapeDtypeStruct((hids, rows, side), jnp.float32),
+            jax.ShapeDtypeStruct((hids, side, rows), jnp.bfloat16),
+        ),
+        in_specs=[vmem] * 2,
+        out_specs=(vmem,) * 3,
+        scratch_shapes=[pltpu.SemaphoreType.DMA((parts,))] * 6,
+        compiler_params=pltpu.CompilerParams(
+            collective_id=1, has_side_effects=True, vmem_limit_bytes=VMEM_BYTES
+        ),
+        cost_estimate=pl.CostEstimate(
+            flops=40 * rows * hid_width,
+            bytes_accessed=8 * rows * hid_width,
+            transcendentals=2 * rows * hid_width,
+        ),
+        name="gather_gelu",
+    )(hidden_pre, out_grad)
+
+
 def local(hidden_pre, out_grad, w_up_blocks, up_index, w_down_blocks, down_index):
     rows, hid_width = hidden_pre.shape
     side = w_up_blocks.shape[1]
@@ -287,15 +365,15 @@
     count = w_down_blocks.shape[0]
     dp_size = lax.axis_size("dp")
     scale = float((rows * dp_size) ** (-0.5))
-    own = out_grad.reshape(rows, -1, side).transpose(1, 0, 2)
-    grads = lax.all_gather(own, "blk", axis=0, tiled=True)
-    feats = grads.shape[0]
-    pre_float = hidden_pre.astype(jnp.float32)
-    normal_cdf = 0.5 * (1.0 + lax.erf(pre_float * inv_root_two))
-    slope = normal_cdf + pre_float * jnp.exp(-0.5 * pre_float * pre_float) * inv_root_twopi
-    slope = slope.reshape(rows, hids, side).transpose(1, 0, 2)
-    acts = (pre_float * normal_cdf).astype(jnp.bfloat16)
-    acts = acts.reshape(rows, hids, side).transpose(1, 2, 0)
+    if lax.axis_size("blk") == 4:
+        feats = 4 * out_grad.shape[1] // side
+        grads, slope, acts = gather_call(hidden_pre, out_grad, side, feats)
+    else:
+        own = out_grad.reshape(rows, -1, side).transpose(1, 0, 2)
+        grads = lax.all_gather(own, "blk", axis=0, tiled=True)
+        acts, slope = gelu_parts(hidden_pre.astype(jnp.float32))
+        slope = slope.reshape(rows, hids, side).transpose(1, 0, 2)
+        acts = acts.reshape(rows, hids, side).transpose(1, 2, 0)
     partial_sum = hidden_call(down_index, up_index, grads, slope, w_down_blocks, w_up_blocks)
     summed = lax.psum_scatter(partial_sum, "blk", scatter_dimension=0, tiled=True)
     summed = summed.transpose(1, 0, 2).reshape(rows, -1)

time: 215 us -> 205 us (0.953)
  waiting for transfers between devices: 17.4 us -> 0.04 us
  Pallas kernels: 163 us -> 180 us
  local copies, waits for them, and re-layouts: 15.5 us -> 9.4 us
  other arithmetic: 3.77 us -> 0 us
    pallas_call x0 -> x1, Pallas kernels: none -> 22.4 us  [gather_call(): pl.pallas_call(functools.partial(gather_kernel, parts), out_shape=(jax.Sh...]
    all_gather x1 -> x0, waiting for transfers between devices: 17.4 us -> none  [local(): grads = lax.all_gather(own, 'blk', axis=0, tiled=True)]
    reshape x2 -> x0, local copies, waits for them, and re-layouts: 4.34 us -> none  [the longest x1 2.83 us: local(): slope = slope.reshape(rows, hids, side).transpose(1, 0, 2)]
    convert_element_type x1 -> x0, other arithmetic: 3.77 us -> none  [local(): acts = (pre_float * normal_cdf).astype(jnp.bfloat16)]
    pallas_call x1, Pallas kernels: 126 us -> 122 us  [weight_call(): pl.pallas_call(functools.partial(weight_kernel, chunks, ahead, scale), ou...]
    convert_element_type x1 -> x0, local copies, waits for them, and re-layouts: 2.82 us -> none  [local(): acts = (pre_float * normal_cdf).astype(jnp.bfloat16)]
    unnamed x7 -> x5, local copies, waits for them, and re-layouts: 4.85 us -> 6.86 us
  transfers between devices with their start and end apart: 2 -> 1, of which waited for: 1 -> 0; matrix products, arithmetic and copies ran while one was open for 5% -> 0% of each run, Pallas kernels for 59% -> 60%
where the time goes in v3:
time: 205 us; the launch traced here: 204 us
  Pallas kernels  180 us (88%)
  between operations  14.1 us (7%)
  local copies, waits for them, and re-layouts  9.4 us (5%)
    pallas_call x1, Pallas kernels, weight_call(): pl.pallas_call(functools.partial(weight_kernel, chunks, ahead, scale), ou...  122 us
    pallas_call x1, Pallas kernels, hidden_call(): pl.pallas_call(functools.partial(hidden_kernel, per_step, group), grid_sp...  35.8 us
    pallas_call x1, Pallas kernels, gather_call(): pl.pallas_call(functools.partial(gather_kernel, parts), out_shape=(jax.Sh...  22.4 us
    unnamed x5, local copies, waits for them, and re-layouts  6.86 us
  transfers between devices with their start and end apart: 1, of which 0 were waited for; matrix products, arithmetic and copies ran while one was open for 0% of the time, Pallas kernels for 60%

profile of v3, /device:TPU:8, one launch (start us, length us, event | category | flops | bytes accessed | tf_op | source)
XLA Modules:
  0.0 203.9 jit_solution(10638756149973427172)
XLA Ops:
  7.2 0.0 reduce-scatter.2.cloned.1.call-start
  7.2 1.5 copy.10.down_ref
  8.7 1.5 copy.11.up_ref
  10.2 22.4 %gather_gelu.1 = (bf16[48,192,128]{2,1,0:T(8,128)(2,1)}, f32[48,192,128]{2,1,0:T(8,128)}, bf16[48,128,192]{2,1,0:T(8,128)(2,1)}) custom-call(bf16[192,6144]{1,0:T(8,128)(2,1)} %hid_ref.1, bf16[192,1536]{1,0:T(8,128)(2,1)} %own_ref.1), custom_call_target="tpu_custom_call" | custom-call | flops 47185920 | bytes 9437184 | tf_op jit(solution)/shard_map/gather_gelu/pallas_call | solution.py:339
  32.6 35.8 %hidden_grads.1 = bf16[48,192,128]{2,1,0:T(8,128)(2,1)} custom-call(s32[288,2]{1,0:T(8,128)} %copy.10.down_ref, s32[288,2]{1,0:T(8,128)} %copy.11.up_ref, bf16[48,192,128]{2,1,0:T(8,128)(2,1)} %get-tuple-element.5.grad_ref, f32[48,192,128]{2,1,0:T(8,128)} %get-tuple-element.6.slope_ref, bf16[288,128,128]{2,1,0:T(8,128)(2,1)} %wd_ref.1, ...), custom_call_target="tpu_custom_call" | custom-call | flops 3623878656 | bytes 18874368 | tf_op jit(solution)/shard_map/hidden_grads/pallas_call | solution.py:80
  68.4 0.0 copy-start
  68.4 0.0 reduce-scatter.2.cloned.1.call-update
  68.4 0.7 copy-done
  69.1 0.6 slice_reduce_fusion
  69.7 122.1 %weight_grads.1 = f32[36,128,128]{2,1,0:T(8,128)} custom-call(s32[288]{0:T(512)} %get-tuple-element.9.hid_ids, s32[288]{0:T(512)} %get-tuple-element.8.feat_ids, bf16[48,128,192]{2,1,0:T(8,128)(2,1)} %get-tuple-element.7.act_ref, bf16[48,192,128]{2,1,0:T(8,128)(2,1)} %get-tuple-element.5.grad_ref), custom_call_target="tpu_custom_call" | custom-call | flops 1811939328 | bytes 18874368 | tf_op jit(solution)/shard_map/weight_grads/pallas_call | solution.py:258
  191.8 0.0 reduce-scatter.2.cloned.1.call-done
  191.8 1.9 copy_bitcast_fusion
  193.8 3.2 %copy.16 = f32[4608,128]{1,0:T(8,128)} copy(f32[4608,128]{1,0:T(8,128)} %bitcast.7) | data formatting | bytes 4718592
Async XLA Ops:
  7.2 184.7 %reduce-scatter.2.cloned.1.call-start = ((), (), s32[]{:S(2)}) async-start(), calls=%async_computation.1 | async-start | bytes 2949120 | tf_op jit(solution)/shard_map/reduce_scatter | solution.py:378
  68.4 0.7 copy-start
Sparse Core Ops, SparseCore 0:
  68.5 33.8 reduce-scatter.1

commit v4 on v3

--- a/solution.py
+++ b/solution.py
@@ -249,10 +249,10 @@
     hids, side, rows = acts.shape
     count = hid_ids.shape[0]
     per = count // (DEEP * WIDE)
-    chunks = chunk_of(per, 6)
+    chunks = chunk_of(per, 9)
     n = per // chunks
     items = DEEP * chunks
-    ahead = min(5, items)
+    ahead = min(8, items)
     slots = pltpu.VMEM((items, n, side, side), jnp.bfloat16)
     sems = pltpu.SemaphoreType.DMA((items,))
     return pl.pallas_call(

time: 205 us -> 204 us (level)
  no operation moved by 1% of the time
where the time goes in v4:
time: 204 us; the launch traced here: 203 us
  Pallas kernels  180 us (88%)
  between operations  14.1 us (7%)
  local copies, waits for them, and re-layouts  9.4 us (5%)
    pallas_call x1, Pallas kernels, weight_call(): pl.pallas_call(functools.partial(weight_kernel, chunks, ahead, scale), ou...  121 us
    pallas_call x1, Pallas kernels, hidden_call(): pl.pallas_call(functools.partial(hidden_kernel, per_step, group), grid_sp...  35.8 us
    pallas_call x1, Pallas kernels, gather_call(): pl.pallas_call(functools.partial(gather_kernel, parts), out_shape=(jax.Sh...  22.4 us
    unnamed x5, local copies, waits for them, and re-layouts  6.86 us
  transfers between devices with their start and end apart: 1, of which 0 were waited for; matrix products, arithmetic and copies ran while one was open for 0% of the time, Pallas kernels for 60%

profile of v4, /device:TPU:8, one launch (start us, length us, event | category | flops | bytes accessed | tf_op | source)
XLA Modules:
  0.0 203.2 jit_solution(15491458242986775648)
XLA Ops:
  7.2 0.0 reduce-scatter.2.cloned.1.call-start
  7.2 1.5 copy.10.down_ref
  8.7 1.5 copy.11.up_ref
  10.2 22.4 %gather_gelu.1 = (bf16[48,192,128]{2,1,0:T(8,128)(2,1)}, f32[48,192,128]{2,1,0:T(8,128)}, bf16[48,128,192]{2,1,0:T(8,128)(2,1)}) custom-call(bf16[192,6144]{1,0:T(8,128)(2,1)} %hid_ref.1, bf16[192,1536]{1,0:T(8,128)(2,1)} %own_ref.1), custom_call_target="tpu_custom_call" | custom-call | flops 47185920 | bytes 9437184 | tf_op jit(solution)/shard_map/gather_gelu/pallas_call | solution.py:339
  32.6 35.8 %hidden_grads.1 = bf16[48,192,128]{2,1,0:T(8,128)(2,1)} custom-call(s32[288,2]{1,0:T(8,128)} %copy.10.down_ref, s32[288,2]{1,0:T(8,128)} %copy.11.up_ref, bf16[48,192,128]{2,1,0:T(8,128)(2,1)} %get-tuple-element.5.grad_ref, f32[48,192,128]{2,1,0:T(8,128)} %get-tuple-element.6.slope_ref, bf16[288,128,128]{2,1,0:T(8,128)(2,1)} %wd_ref.1, ...), custom_call_target="tpu_custom_call" | custom-call | flops 3623878656 | bytes 18874368 | tf_op jit(solution)/shard_map/hidden_grads/pallas_call | solution.py:80
  68.4 0.0 copy-start
  68.4 0.0 reduce-scatter.2.cloned.1.call-update
  68.4 0.7 copy-done
  69.1 0.6 slice_reduce_fusion
  69.7 121.5 %weight_grads.1 = f32[36,128,128]{2,1,0:T(8,128)} custom-call(s32[288]{0:T(512)} %get-tuple-element.9.hid_ids, s32[288]{0:T(512)} %get-tuple-element.8.feat_ids, bf16[48,128,192]{2,1,0:T(8,128)(2,1)} %get-tuple-element.7.act_ref, bf16[48,192,128]{2,1,0:T(8,128)(2,1)} %get-tuple-element.5.grad_ref), custom_call_target="tpu_custom_call" | custom-call | flops 1811939328 | bytes 18874368 | tf_op jit(solution)/shard_map/weight_grads/pallas_call | solution.py:258
  191.2 0.0 reduce-scatter.2.cloned.1.call-done
  191.2 1.9 copy_bitcast_fusion
  193.1 3.2 %copy.16 = f32[4608,128]{1,0:T(8,128)} copy(f32[4608,128]{1,0:T(8,128)} %bitcast.7) | data formatting | bytes 4718592
Async XLA Ops:
  7.2 184.0 %reduce-scatter.2.cloned.1.call-start = ((), (), s32[]{:S(2)}) async-start(), calls=%async_computation.1 | async-start | bytes 2949120 | tf_op jit(solution)/shard_map/reduce_scatter | solution.py:378
  68.4 0.7 copy-start
Sparse Core Ops, SparseCore 0:
  68.5 33.8 reduce-scatter.1
